TPU v7x, 32 devices: a whole 2x2x4 slice. The times are simulated.
32 devices in a mesh: groups: 2 (over y), sector: 8 (over z, x), term: 2 (over core).
Axes of the slice: x: 2, y: 2, z: 4, core: 2. Of those that a mesh axis runs over, the one named last changes fastest.
Arguments:
- psi_tiles: bfloat16 [16, 16, 256, 128], P(('groups', 'sector')), parts along dimension 0, may hold values from -6 to 6
- env_left: bfloat16 [16, 34, 256, 256], P(('groups', 'sector'), 'term'), parts along dimension 0, may hold values from -0.375 to 0.375
- env_right: bfloat16 [16, 34, 128, 128], P(('groups', 'sector'), 'term'), parts along dimension 0, may hold values from -0.5 to 0.5
- mpo_local: bfloat16 [68, 16, 16], P(('groups', 'term')), parts along dimension 0, may hold values from -0.25 to 0.25
- term_class: int32 [68], P(('groups', 'term')), parts along dimension 0, may hold values from 0 to 4
Outputs:
- h_psi: bfloat16 [16, 16, 256, 128], P(('groups', 'sector'), 'term'), parts along dimension 0
There are 2 independent parts, one for each index of `groups`. A program takes and returns all parts, laid end to end along the dimension named above; each array names one. Nothing has to cross between parts.
All inputs are finite; a program needn't handle non-finite values.
Results may differ from a plain program's by a relative error of at most 0.0057.
Values may be sent and summed in bfloat16 or wider, within the bound.
A program may use at most 64 MiB of HBM per device.

v0:
```python
import jax
import jax.numpy as jnp
from jax import lax
from jax.sharding import PartitionSpec as P

GRID = 4


def extended(cells, sides, width):
    for axis, dim in sides:
        count = lax.axis_size(axis)
        ends = count - 1
        head = lax.slice_in_dim(cells, 0, width, axis=dim)
        tail = lax.slice_in_dim(cells, cells.shape[dim] - width, cells.shape[dim], axis=dim)
        cells = jnp.concatenate(
            [
                lax.ppermute(tail, axis, [(i, (i + 1) % count) for i in range(ends)]),
                cells,
                lax.ppermute(head, axis, [((i + 1) % count, i) for i in range(ends)]),
            ],
            axis=dim,
        )
    return cells


def passed_along(value, axis, steps):
    count = lax.axis_size(axis)
    leading, last = (max(0, -steps), min(count, count - steps))
    return lax.ppermute(value, axis, [(source, source + steps) for source in range(leading, last)])


def shards(psi_tiles, env_left, env_right, mpo_local, term_class):
    column = (lax.axis_index("sector") + 1) % GRID
    padded = extended(psi_tiles, (("sector", 0),), 1)
    lower = passed_along(psi_tiles, "sector", GRID)
    upper = passed_along(psi_tiles, "sector", -GRID)
    before, after = (padded[0], padded[2])
    lower, upper = (lower[0], upper[0])
    before = jnp.where(column > 0, before, jnp.zeros_like(before))
    after = jnp.where(column < GRID - 1, after, jnp.zeros_like(after))
    candidates = jnp.stack([psi_tiles[0], before, after, lower, upper], 0)
    states, rows, width = (psi_tiles.shape[1], psi_tiles.shape[2], psi_tiles.shape[3])
    lefts, rights = (env_left[0], env_right[0])

    def add_term(index, total):
        source = lax.dynamic_index_in_dim(candidates, term_class[index], 0, keepdims=False)
        right_part = jnp.dot(
            source.reshape(states * rows, width), rights[index], preferred_element_type=jnp.float32
        )
        right_part = right_part.astype(jnp.bfloat16).reshape(states, rows * width)
        mixed = jnp.dot(mpo_local[index], right_part, preferred_element_type=jnp.float32)
        mixed = mixed.astype(jnp.bfloat16).reshape(states, rows, width)
        term_part = lax.dot_general(
            lefts[index], mixed, (((1,), (1,)), ((), ())), preferred_element_type=jnp.float32
        )
        return total + term_part

    start = jnp.zeros((rows, states, width), jnp.float32)
    total = lax.fori_loop(0, mpo_local.shape[0], add_term, start)
    total = jnp.transpose(total, (1, 0, 2))[None]
    return lax.psum_scatter(total, "term", scatter_dimension=1, tiled=True).astype(jnp.bfloat16)


def solution(mesh):
    placed = (
        P(("groups", "sector"), None, None, None),
        P(("groups", "sector"), "term", None, None),
        P(("groups", "sector"), "term", None, None),
        P(("groups", "term"), None, None),
        P(("groups", "term")),
    )
    return jax.shard_map(
        shards,
        mesh=mesh,
        in_specs=placed,
        out_specs=P(("groups", "sector"), "term", None, None),
        check_vma=False,
    )
```

profile of v0, /device:TPU:9, one launch (start us, length us, event | category | flops | bytes accessed | tf_op | source)
XLA Modules:
  0.0 278.6 jit_solution(7298939993019139649)
XLA Ops:
  6.5 3.1 %collective-permute-start = (bf16[1,16,256,128]{3,2,1,0:T(8,128)(2,1)}, bf16[1,16,256,128]{3,2,1,0:T(8,128)(2,1)S(1)}, u32[]{:S(2)}, u32[]{:S(2)}) collective-permute-start(bf16[1,16,256,128]{3,2,1,0:T(8,128)(2,1)} %param.7), channel_id=1, source_target_pairs={{0,2},{2,4},{4,6},{6,8},{8,10},{10,12},{12,14},{1,3},{3,5},{5,7},{... | collective-permute-start | bytes 3145736 | tf_op jit(solution)/shard_map/ppermute | solution.py:17
  9.7 3.1 %collective-permute-start.1 = (bf16[1,16,256,128]{3,2,1,0:T(8,128)(2,1)}, bf16[1,16,256,128]{3,2,1,0:T(8,128)(2,1)S(1)}, u32[]{:S(2)}, u32[]{:S(2)}) collective-permute-start(bf16[1,16,256,128]{3,2,1,0:T(8,128)(2,1)} %param.7), channel_id=1, source_target_pairs={{2,0},{4,2},{6,4},{8,6},{10,8},{12,10},{14,12},{3,1},{5,3},{7,5},{... | collective-permute-start | bytes 3145736 | tf_op jit(solution)/shard_map/ppermute | solution.py:19
  12.7 5.2 %collective-permute-start.2 = (bf16[1,16,256,128]{3,2,1,0:T(8,128)(2,1)}, bf16[1,16,256,128]{3,2,1,0:T(8,128)(2,1)}, u32[]{:S(2)}, u32[]{:S(2)}) collective-permute-start(bf16[1,16,256,128]{3,2,1,0:T(8,128)(2,1)} %param.7), channel_id=1, source_target_pairs={{0,8},{2,10},{4,12},{6,14},{1,9},{3,11},{5,13},{7,15},{16,24},{18,... | collective-permute-start | bytes 3145736 | tf_op jit(solution)/shard_map/ppermute | solution.py:29
  21.6 32.5 %collective-permute-done = bf16[1,16,256,128]{3,2,1,0:T(8,128)(2,1)S(1)} collective-permute-done((bf16[1,16,256,128]{3,2,1,0:T(8,128)(2,1)}, bf16[1,16,256,128]{3,2,1,0:T(8,128)(2,1)S(1)}, u32[]{:S(2)}, u32[]{:S(2)}) %collective-permute-start) | collective-permute-done | bytes 1048608 | tf_op jit(solution)/shard_map/ppermute | solution.py:17
  54.4 2.7 collective-permute-done.1
  57.4 5.1 %collective-permute-done.2 = bf16[1,16,256,128]{3,2,1,0:T(8,128)(2,1)} collective-permute-done((bf16[1,16,256,128]{3,2,1,0:T(8,128)(2,1)}, bf16[1,16,256,128]{3,2,1,0:T(8,128)(2,1)}, u32[]{:S(2)}, u32[]{:S(2)}) %collective-permute-start.2) | collective-permute-done | bytes 1048608 | tf_op jit(solution)/shard_map/ppermute | solution.py:29
  62.5 1.4 constant_dynamic-update-slice_fusion.1
  64.0 2.3 copy-done.2
  66.3 175.7 %while.14 = (s32[]{:T(128)}, f32[256,16,128]{2,0,1:T(8,128)}, bf16[17,256,256]{2,1,0:T(8,128)(2,1)}, bf16[17,16,16]{2,1,0:T(8,128)(2,1)S(1)}, s32[17]{0:T(128)S(...) while((s32[]{:T(128)}, f32[256,16,128]{2,0,1:T(8,128)}, ...), condition=%wide.region_1.2_spmd.clone, body=%wide.region_0.1_spmd.clone.sunk | while | flops 421527552 | bytes 32675036 | solution.py:59
  73.6 1.7 select_add_fusion.2
  83.9 1.7 select_add_fusion.2
  94.3 1.7 select_add_fusion.2
  104.6 1.7 select_add_fusion.2
  106.3 1.3 copy-done.1
  114.9 1.7 select_add_fusion.2
  125.3 1.7 select_add_fusion.2
  127.0 1.3 copy-done.1
  135.6 1.7 select_add_fusion.2
  137.3 1.3 copy-done.1
  145.9 1.7 select_add_fusion.2
  147.7 1.3 copy-done.1
  156.3 1.7 select_add_fusion.2
  166.6 1.7 select_add_fusion.2
  176.9 1.7 select_add_fusion.2
  187.3 1.7 select_add_fusion.2
  197.6 1.7 select_add_fusion.2
  207.9 1.7 select_add_fusion.2
  218.3 1.7 select_add_fusion.2
  228.6 1.7 select_add_fusion.2
  238.9 1.7 select_add_fusion.2
  242.0 27.6 %reduce-scatter.2.cloned.1.call-done = f32[1,8,256,128]{3,2,1,0:T(8,128)} async-done(((f32[1,16,256,128]{3,2,1,0:T(8,128)}), f32[1,8,256,128]{3,2,1,0:T(8,128)}) %reduce-scatter.2.cloned.1.call-update) | async-done | bytes 1048592 | tf_op jit(solution)/shard_map/reduce_scatter | solution.py:61
  269.7 2.1 convert_element_type.17
  (179 shorter events, 110.0 us)
Async XLA Ops:
  6.5 263.1 %reduce-scatter.2.cloned.1.call-start = ((), (), s32[]{:S(2)}) async-start(), calls=%async_computation.1 | async-start | bytes 3145728 | tf_op jit(solution)/shard_map/reduce_scatter | solution.py:61
  6.5 47.6 %collective-permute-start = (bf16[1,16,256,128]{3,2,1,0:T(8,128)(2,1)}, bf16[1,16,256,128]{3,2,1,0:T(8,128)(2,1)S(1)}, u32[]{:S(2)}, u32[]{:S(2)}) collective-permute-start(bf16[1,16,256,128]{3,2,1,0:T(8,128)(2,1)} %param.7), channel_id=1, source_target_pairs={{0,2},{2,4},{4,6},{6,8},{8,10},{10,12},{12,14},{1,3},{3,5},{5,7},{... | collective-permute-start | bytes 3145736 | tf_op jit(solution)/shard_map/ppermute | solution.py:17
  9.7 47.4 %collective-permute-start.1 = (bf16[1,16,256,128]{3,2,1,0:T(8,128)(2,1)}, bf16[1,16,256,128]{3,2,1,0:T(8,128)(2,1)S(1)}, u32[]{:S(2)}, u32[]{:S(2)}) collective-permute-start(bf16[1,16,256,128]{3,2,1,0:T(8,128)(2,1)} %param.7), channel_id=1, source_target_pairs={{2,0},{4,2},{6,4},{8,6},{10,8},{12,10},{14,12},{3,1},{5,3},{7,5},{... | collective-permute-start | bytes 3145736 | tf_op jit(solution)/shard_map/ppermute | solution.py:19
  12.7 49.8 %collective-permute-start.2 = (bf16[1,16,256,128]{3,2,1,0:T(8,128)(2,1)}, bf16[1,16,256,128]{3,2,1,0:T(8,128)(2,1)}, u32[]{:S(2)}, u32[]{:S(2)}) collective-permute-start(bf16[1,16,256,128]{3,2,1,0:T(8,128)(2,1)} %param.7), channel_id=1, source_target_pairs={{0,8},{2,10},{4,12},{6,14},{1,9},{3,11},{5,13},{7,15},{16,24},{18,... | collective-permute-start | bytes 3145736 | tf_op jit(solution)/shard_map/ppermute | solution.py:29
  17.9 46.0 %collective-permute-start.3 = (bf16[1,16,256,128]{3,2,1,0:T(8,128)(2,1)}, bf16[1,16,256,128]{3,2,1,0:T(8,128)(2,1)S(1)}, u32[]{:S(2)}, u32[]{:S(2)}) collective-permute-start(bf16[1,16,256,128]{3,2,1,0:T(8,128)(2,1)} %param.7), channel_id=1, source_target_pairs={{8,0},{10,2},{12,4},{14,6},{9,1},{11,3},{13,5},{15,7},{24,16},{26,... | collective-permute-start | bytes 3145736 | tf_op jit(solution)/shard_map/ppermute | solution.py:29
  20.2 46.1 %copy-start.3 = (s32[17]{0:T(128)S(1)}, s32[17]{0:T(128)}, u32[]{:S(2)}) copy-start(s32[17]{0:T(128)} %param.11) | copy-start | bytes 208
  64.0 2.3 copy-start.2
  72.0 1.6 copy-start
  75.3 1.3 copy-start.1
  82.4 1.6 copy-start
  92.7 1.6 copy-start
  96.0 1.3 copy-start.1
  103.0 1.6 copy-start
  106.3 1.3 copy-start.1
  113.4 1.6 copy-start
  123.7 1.6 copy-start
  127.0 1.3 copy-start.1
  134.0 1.6 copy-start
  137.3 1.3 copy-start.1
  144.4 1.6 copy-start
  147.6 1.3 copy-start.1
  154.7 1.6 copy-start
  158.0 1.3 copy-start.1
  165.0 1.6 copy-start
  168.3 1.3 copy-start.1
  175.4 1.6 copy-start
  185.7 1.6 copy-start
  196.0 1.6 copy-start
  206.3 1.6 copy-start
  216.7 1.6 copy-start
  227.0 1.6 copy-start
  237.3 1.6 copy-start
  (9 other events, 12.1 us)
Sparse Core Ops, SparseCore 0:
  242.1 27.4 reduce-scatter.1
where the time goes:
time: 283 us; the launch traced here: 279 us
  local copies, waits for them, and re-layouts  89.9 us (32%)
  waiting for transfers between devices  67.9 us (24%)
  matrix products  56 us (20%)
  loops' own time  35.9 us (13%)
  between operations  13.5 us (5%)
  starting transfers between devices  12.6 us (4%)
    while x85, local copies, waits for them, and re-layouts  42.2 us
    another operation x1, loops' own time, shards(): total = lax.fori_loop(0, mpo_local.shape[0], add_term, start)  35.9 us
    ppermute x1, waiting for transfers between devices, extended(): lax.ppermute(tail, axis, [(i, (i + 1) % count) for i in range(ends)])  32.5 us
    dot_general x17, matrix products, add_term(): lax.dot_general(lefts[index], mixed, (((1,), (1,)), ((), ())), preferred_...  28.9 us
    reduce_scatter x1, waiting for transfers between devices, shards(): lax.psum_scatter(total, 'term', scatter_dimension=1, tiled=True)  27.6 us
    dynamic_slice x17, local copies, waits for them, and re-layouts, add_term(): lax.dynamic_index_in_dim(candidates, term_class[index], 0, keepdims=False)  22.1 us
    dot_general x17, matrix products, add_term(): jnp.dot(source.reshape(states * rows, width), rights[index], preferred_el...  20.1 us
    dynamic_slice x17, local copies, waits for them, and re-layouts, add_term(): term_class[index]  11 us
  transfers between devices with their start and end apart: 5, of which 4 were waited for; matrix products, arithmetic and copies ran while one was open for 2% of the time, Pallas kernels for 0%

commit v1 on v0

v1 whole, which is shorter than its diff:
```python
import functools

import jax
import jax.numpy as jnp
from jax import lax
from jax.experimental import pallas as pl
from jax.experimental.pallas import tpu as pltpu
from jax.sharding import PartitionSpec as P

GRID = 4
MESH = pl.DeviceIdType.MESH
STEPS = (-1, 1, -GRID, GRID)
VMEM_LIMIT = 56 * 1024 * 1024


def has_source(sector, sectors, step):
    column = lax.rem(sector + 1, GRID)
    if step == -1:
        return (sector >= 1) & (column > 0)
    if step == 1:
        return (sector + 1 < sectors) & (column < GRID - 1)
    if step < 0:
        return sector + step >= 0
    return sector + step < sectors


def exchange_kernel(sectors, psi_ref, out_ref, send_sem, recv_sem, pass_sem, got_sem):
    group, sector, core = (lax.axis_index(name) for name in ("groups", "sector", "term"))
    half = psi_ref.shape[0] // 2
    mine = pl.ds(core * half, half)
    barrier = pltpu.get_barrier_semaphore()
    sibling = (group, sector, 1 - core)
    count = jnp.int32(1)
    pl.semaphore_signal(barrier, inc=1, device_id=sibling, device_id_type=MESH)
    for step in STEPS:
        there = has_source(sector, sectors, step)
        count = count + there.astype(jnp.int32)

        @pl.when(there)
        def _():
            pl.semaphore_signal(barrier, inc=1, device_id=(group, sector + step, core), device_id_type=MESH)

    pl.semaphore_wait(barrier, count)

    def outgoing(slot):
        step = STEPS[slot]
        return pltpu.make_async_remote_copy(
            src_ref=psi_ref.at[mine],
            dst_ref=out_ref.at[slot, mine],
            send_sem=send_sem.at[slot],
            recv_sem=recv_sem.at[slot],
            device_id=(group, sector - step, core),
            device_id_type=MESH,
        )

    def passing(slot):
        return pltpu.make_async_remote_copy(
            src_ref=out_ref.at[slot, mine],
            dst_ref=out_ref.at[slot, mine],
            send_sem=pass_sem.at[slot],
            recv_sem=got_sem.at[slot],
            device_id=sibling,
            device_id_type=MESH,
        )

    there = [has_source(sector, sectors, step) for step in STEPS]
    wanted = [has_source(sector, sectors, -step) for step in STEPS]
    for slot in range(len(STEPS)):
        pl.when(wanted[slot])(lambda slot=slot: outgoing(slot).start())
    for slot in range(len(STEPS)):

        @pl.when(there[slot])
        def _():
            outgoing(slot).wait_recv()
            passing(slot).start()

    for slot in range(len(STEPS)):

        @pl.when(there[slot])
        def _():
            passing(slot).wait()

        pl.when(wanted[slot])(lambda slot=slot: outgoing(slot).wait_send())


def exchange(psi, sectors):
    slots = len(STEPS)
    return pl.pallas_call(
        functools.partial(exchange_kernel, sectors),
        out_shape=jax.ShapeDtypeStruct((slots, *psi.shape), psi.dtype),
        in_specs=[pl.BlockSpec(memory_space=pl.ANY)],
        out_specs=pl.BlockSpec(memory_space=pl.ANY),
        scratch_shapes=[pltpu.SemaphoreType.DMA((slots,))] * 4,
        compiler_params=pltpu.CompilerParams(collective_id=0, has_side_effects=True, vmem_limit_bytes=VMEM_LIMIT),
        name="exchange",
    )(psi)


def add_pair(xs, rights, mpos, lefts, scales, held, mixed, acc, first):
    states, rows, width = acc.shape
    step = 16
    wide = states * step
    index = lambda axis: lax.broadcasted_iota(jnp.int32, (wide, wide), axis)
    same = lax.rem(index(0), step) == lax.rem(index(1), step)
    spread = (lax.broadcasted_iota(jnp.int32, (wide, states), 0) // step
              == lax.broadcasted_iota(jnp.int32, (wide, states), 1)).astype(jnp.bfloat16)
    spread_t = (lax.broadcasted_iota(jnp.int32, (states, wide), 1) // step
                == lax.broadcasted_iota(jnp.int32, (states, wide), 0)).astype(jnp.bfloat16)

    def dot(a, b):
        return jnp.dot(a, b, preferred_element_type=jnp.float32)

    krons = []
    for mpo, scale in zip(mpos, scales):
        tall = dot(spread, mpo).astype(jnp.bfloat16)
        krons.append(jnp.where(same, dot(tall, spread_t) * scale, 0.0).astype(jnp.bfloat16))
    zero = jnp.zeros((width, width), jnp.bfloat16)
    right = jnp.concatenate(
        [jnp.concatenate([rights[0], zero], 1), jnp.concatenate([zero, rights[1]], 1)], 0
    )
    for s in range(0, states, 2):
        x = jnp.concatenate([x(s).reshape(2 * rows, width) for x in xs], 1)
        held[pl.ds(s, 2)] = dot(x, right).astype(jnp.bfloat16).reshape(2, rows, 2 * width)
    for t in range(2):
        for r in range(0, rows, 2 * step):
            part = [
                held[:, pl.ds(r + o, step), pl.ds(t * width, width)].reshape(wide, width) for o in (0, step)
            ]
            out = dot(krons[t], jnp.concatenate(part, 1)).astype(jnp.bfloat16)
            for n, o in enumerate((0, step)):
                mixed[t, :, pl.ds(r + o, step), :] = out[:, n * width:(n + 1) * width].reshape(states, step, width)
    left = jnp.concatenate(lefts, 1)
    for s in range(0, states, 2):
        part = [jnp.concatenate([mixed[t, s], mixed[t, s + 1]], 1) for t in range(2)]
        out = dot(left, jnp.concatenate(part, 0))
        for n in range(2):
            acc[s + n] += out[:, n * width:(n + 1) * width]


def terms_kernel(plan_ref, scale_ref, psi_ref, got_ref, left_ref, right_ref, mpo_ref, out_ref,
                 tiles, lefts, acc, held, mixed, sems):
    terms = left_ref.shape[0]
    copies = [
        pltpu.make_async_copy(psi_ref, tiles.at[0], sems.at[0]),
        pltpu.make_async_copy(got_ref, tiles.at[pl.ds(1, got_ref.shape[0])], sems.at[1]),
        pltpu.make_async_copy(left_ref, lefts, sems.at[2]),
    ]
    for copy in copies:
        copy.start()
    acc[...] = jnp.zeros_like(acc)
    for copy in copies:
        copy.wait()
    pairs = plan_ref[2, 0]

    @pl.loop(0, pairs)
    def _(pair):
        term = [plan_ref[0, 2 * pair + t] for t in range(2)]
        kind = [plan_ref[1, 2 * pair + t] for t in range(2)]
        add_pair(
            [lambda s, k=k: tiles[k, pl.ds(s, 2)] for k in kind],
            [right_ref[i] for i in term],
            [mpo_ref[i] for i in term],
            [lefts[i] for i in term],
            [scale_ref[2 * pair + t] for t in range(2)],
            held, mixed, acc, None,
        )

    out_ref[...] = acc[...]


def all_terms(plan, scale, psi, got, left, right, mpo):
    states, rows, width = psi.shape
    slots = got.shape[0]
    any_spec = pl.BlockSpec(memory_space=pl.ANY)
    smem = pl.BlockSpec(memory_space=pltpu.SMEM)
    vmem = pl.BlockSpec(memory_space=pltpu.VMEM)
    return pl.pallas_call(
        terms_kernel,
        out_shape=jax.ShapeDtypeStruct(psi.shape, jnp.float32),
        in_specs=[smem, smem, any_spec, any_spec, any_spec, vmem, vmem],
        out_specs=vmem,
        scratch_shapes=[
            pltpu.VMEM((slots + 1, states, rows, width), jnp.bfloat16),
            pltpu.VMEM(left.shape, jnp.bfloat16),
            pltpu.VMEM((states, rows, width), jnp.float32),
            pltpu.VMEM((states, rows, 2 * width), jnp.bfloat16),
            pltpu.VMEM((2, states, rows, width), jnp.bfloat16),
            pltpu.SemaphoreType.DMA((3,)),
        ],
        compiler_params=pltpu.CompilerParams(vmem_limit_bytes=VMEM_LIMIT),
        name="terms",
    )(plan, scale, psi, got, left, right, mpo)


def join_kernel(total_ref, out_ref, inbox, sems):
    group, sector, core = (lax.axis_index(name) for name in ("groups", "sector", "term"))
    half = out_ref.shape[0]
    sibling = (group, sector, 1 - core)
    barrier = pltpu.get_barrier_semaphore()
    pl.semaphore_signal(barrier, inc=1, device_id=sibling, device_id_type=MESH)
    pl.semaphore_wait(barrier, 1)
    copy = pltpu.make_async_remote_copy(
        src_ref=total_ref.at[pl.ds((1 - core) * half, half)],
        dst_ref=inbox,
        send_sem=sems.at[0],
        recv_sem=sems.at[1],
        device_id=sibling,
        device_id_type=MESH,
    )
    copy.start()
    copy.wait()
    out_ref[...] = (total_ref[pl.ds(core * half, half)] + inbox[...]).astype(out_ref.dtype)


def joined(total):
    states, rows, width = total.shape
    return pl.pallas_call(
        join_kernel,
        out_shape=jax.ShapeDtypeStruct((states // 2, rows, width), jnp.bfloat16),
        in_specs=[pl.BlockSpec(memory_space=pltpu.VMEM)],
        out_specs=pl.BlockSpec(memory_space=pltpu.VMEM),
        scratch_shapes=[
            pltpu.VMEM((states // 2, rows, width), jnp.float32),
            pltpu.SemaphoreType.DMA((2,)),
        ],
        compiler_params=pltpu.CompilerParams(collective_id=1, has_side_effects=True, vmem_limit_bytes=VMEM_LIMIT),
        name="join",
    )(total)


def planned(term_class, sectors):
    sector = lax.axis_index("sector")
    there = jnp.stack([jnp.bool_(True)] + [has_source(sector, sectors, step) for step in STEPS])
    kinds = jnp.arange(len(STEPS) + 1)
    exists = jnp.any((term_class[:, None] == kinds) & there, 1)
    count = term_class.shape[0]
    number = jnp.arange(count)
    key = jnp.where(exists, term_class, len(STEPS) + 1) * count + number
    rank = jnp.sum(key[None, :] < key[:, None], 1)
    valid = jnp.sum(exists.astype(jnp.int32))
    place = jnp.arange(count + 1)
    at = (rank[None, :] == place[:, None]) & exists
    term = jnp.sum(jnp.where(at, number, 0), 1)
    kind = jnp.sum(jnp.where(at, term_class, 0), 1)
    pairs = jnp.broadcast_to((valid + 1) // 2, place.shape)
    plan = jnp.stack([term, kind, pairs]).astype(jnp.int32)
    return plan, (place < valid).astype(jnp.float32)


def shards(psi_tiles, env_left, env_right, mpo_local, term_class):
    sectors = lax.axis_size("sector")
    plan, scale = planned(term_class, sectors)
    got = exchange(psi_tiles[0], sectors)
    total = all_terms(plan, scale, psi_tiles[0], got, env_left[0], env_right[0], mpo_local)
    return joined(total)[None]


def solution(mesh):
    placed = (
        P(("groups", "sector"), None, None, None),
        P(("groups", "sector"), "term", None, None),
        P(("groups", "sector"), "term", None, None),
        P(("groups", "term"), None, None),
        P(("groups", "term")),
    )
    return jax.shard_map(
        shards,
        mesh=mesh,
        in_specs=placed,
        out_specs=P(("groups", "sector"), "term", None, None),
        check_vma=False,
    )
```

time: 283 us -> 74.4 us (0.26)
  the two profiles are of different devices: /device:TPU:9 before, /device:TPU:5 now
where the time goes in v1:
time: 74.4 us; the launch traced here: 73.8 us
  Pallas kernels  64.6 us (87%)
  other arithmetic  4.84 us (7%)
  local copies, waits for them, and re-layouts  3.69 us (5%)
    pallas_call x1, Pallas kernels, exchange(): pl.pallas_call(functools.partial(exchange_kernel, sectors), out_shape=jax...  41.1 us
    pallas_call x1, Pallas kernels, all_terms(): pl.pallas_call(terms_kernel, out_shape=jax.ShapeDtypeStruct(psi.shape, jn...  18.3 us
    pallas_call x1, Pallas kernels, joined(): pl.pallas_call(join_kernel, out_shape=jax.ShapeDtypeStruct((states // 2,...  5.17 us
    unnamed x2, local copies, waits for them, and re-layouts  3.52 us

profile of v1, /device:TPU:5, one launch (start us, length us, event | category | flops | bytes accessed | tf_op | source)
XLA Modules:
  0.0 73.8 jit_solution(13994368038272786703)
XLA Ops:
  0.0 0.1 stack.28
  0.1 0.7 %fusion.2 = pred[17]{0:T(512)(128)(4,1)S(1)} fusion(s32[17]{0:T(128)} %param.9, pred[5]{0:T(512)(128)(4,1)S(1)} %stack.28), kind=kLoop, calls=%fused_computation.7 | loop fusion | flops 238 | bytes 90 | tf_op jit(solution)/shard_map/reduce_or | solution.py:235
  0.8 1.3 %convert_reduce_fusion.1 = (s32[]{:T(128)}, s32[17]{0:T(128)S(1)}) fusion(pred[17]{0:T(512)(128)(4,1)S(1)} %fusion.2, s32[17]{0:T(128)} %param.9), kind=kLoop, calls=%fused_computation.10 | loop fusion | flops 84 | bytes 157 | tf_op jit(solution)/shard_map/reduce_sum | solution.py:240
  2.8 0.2 convert_reduce_fusion
  3.0 0.1 pad.2.clone
  3.1 0.8 %select_reduce_fusion.1 = (s32[18]{0:T(128)S(1)}, s32[18]{0:T(128)S(1)}) fusion(s32[17]{0:T(128)S(1)} %convert_reduce_fusion, pred[17]{0:T(512)(128)(4,1)S(1)} %fusion.2, s32[17]{0:T(128)} %param.9), kind=kLoop, calls=%fused_computation.1 | loop fusion | flops 1800 | bytes 297 | tf_op jit(solution)/shard_map/reduce_sum | solution.py:243
  3.8 0.7 add_add_fusion.plan_ref
  4.5 1.2 %compare_convert_fusion.scale_ref = f32[18]{0:T(128)} fusion(s32[]{:T(128)} %get-tuple-element.7), kind=kLoop, calls=%fused_computation.9 | loop fusion | flops 36 | bytes 76 | tf_op jit(solution)/shard_map/convert_element_type | solution.py:247
  5.7 1.6 %copy.7.mpo_ref = bf16[17,16,16]{2,1,0:T(8,128)(2,1)} copy(bf16[17,16,16]{0,2,1:T(8,128)(2,1)} %param.8) | data formatting | bytes 17408 | tf_op args[3]
  7.3 41.1 %exchange.1.got_ref = bf16[4,16,256,128]{3,2,1,0:T(8,128)(2,1)} custom-call(bf16[16,256,128]{2,1,0:T(8,128)(2,1)} %bitcast.11), custom_call_target="tpu_custom_call" | custom-call | tf_op jit(solution)/shard_map/exchange/pallas_call | solution.py:88
  48.4 18.3 %terms.1.total_ref = f32[16,256,128]{2,1,0:T(8,128)} custom-call(s32[3,18]{1,0:T(4,128)} %add_add_fusion.plan_ref, f32[18]{0:T(128)} %compare_convert_fusion.scale_ref, bf16[16,256,128]{2,1,0:T(8,128)(2,1)} %bitcast.12, bf16[4,16,256,128]{3,2,1,0:T(8,128)(2,1)} %exchange.1.got_ref, bf16[17,256,256]{2,1,0:T(8,128)(2,1)} %bitcast.13, ...), custom_call_target="tpu_custom_call" | custom-call | tf_op jit(solution)/shard_map/terms/pallas_call | solution.py:177
  66.8 5.2 %join.1 = bf16[8,256,128]{2,1,0:T(8,128)(2,1)} custom-call(f32[16,256,128]{2,1,0:T(8,128)} %terms.1.total_ref), custom_call_target="tpu_custom_call" | custom-call | tf_op jit(solution)/shard_map/join/pallas_call | solution.py:217
  71.9 1.9 %copy.9 = bf16[1,8,256,128]{3,2,1,0:T(8,128)(2,1)} copy(bf16[1,8,256,128]{3,2,1,0:T(8,128)(2,1)} %bitcast.14) | data formatting | bytes 1048576

commit v2 on v0

v2 whole, which is shorter than its diff:
```python
import functools

import jax
import jax.numpy as jnp
from jax import lax
from jax.experimental import pallas as pl
from jax.experimental.pallas import tpu as pltpu
from jax.sharding import PartitionSpec as P

GRID = 4
MESH = pl.DeviceIdType.MESH
STEPS = (-1, 1, -GRID, GRID)
FRONT_KINDS, FRONT_SLOTS = 3, 6
VMEM_LIMIT = 56 * 1024 * 1024


def has_source(sector, sectors, step):
    column = lax.rem(sector + 1, GRID)
    if step == -1:
        return (sector >= 1) & (column > 0)
    if step == 1:
        return (sector + 1 < sectors) & (column < GRID - 1)
    if step < 0:
        return sector + step >= 0
    return sector + step < sectors


def add_pair(xs, rights, mpos, lefts, scales, held, mixed, acc):
    states, rows, width = acc.shape
    step = 16
    wide = states * step
    index = lambda axis: lax.broadcasted_iota(jnp.int32, (wide, wide), axis)
    same = lax.rem(index(0), step) == lax.rem(index(1), step)
    spread = (lax.broadcasted_iota(jnp.int32, (wide, states), 0) // step
              == lax.broadcasted_iota(jnp.int32, (wide, states), 1)).astype(jnp.bfloat16)
    spread_t = (lax.broadcasted_iota(jnp.int32, (states, wide), 1) // step
                == lax.broadcasted_iota(jnp.int32, (states, wide), 0)).astype(jnp.bfloat16)

    def dot(a, b):
        return jnp.dot(a, b, preferred_element_type=jnp.float32)

    krons = []
    for mpo, scale in zip(mpos, scales):
        tall = dot(spread, mpo).astype(jnp.bfloat16)
        krons.append(jnp.where(same, dot(tall, spread_t) * scale, 0.0).astype(jnp.bfloat16))
    zero = jnp.zeros((width, width), jnp.bfloat16)
    right = jnp.concatenate(
        [jnp.concatenate([rights[0], zero], 1), jnp.concatenate([zero, rights[1]], 1)], 0
    )
    for s in range(0, states, 2):
        x = jnp.concatenate([x(s).reshape(2 * rows, width) for x in xs], 1)
        held[pl.ds(s, 2)] = dot(x, right).astype(jnp.bfloat16).reshape(2, rows, 2 * width)
    for t in range(2):
        for r in range(0, rows, 2 * step):
            part = [
                held[:, pl.ds(r + o, step), pl.ds(t * width, width)].reshape(wide, width) for o in (0, step)
            ]
            out = dot(krons[t], jnp.concatenate(part, 1)).astype(jnp.bfloat16)
            for n, o in enumerate((0, step)):
                mixed[t, :, pl.ds(r + o, step), :] = out[:, n * width:(n + 1) * width].reshape(states, step, width)
    left = jnp.concatenate(lefts, 1)
    for s in range(0, states, 2):
        part = [jnp.concatenate([mixed[t, s], mixed[t, s + 1]], 1) for t in range(2)]
        out = dot(left, jnp.concatenate(part, 0))
        for n in range(2):
            acc[s + n] += out[:, n * width:(n + 1) * width]


def front_kernel(sectors, class_ref, psi_ref, left_ref, right_ref, mpo_ref, got_ref, acc,
                 tiles, lefts, rights, held, mixed, plan, send_sem, recv_sem, pass_sem, got_sem, local_sem):
    group, sector, core = (lax.axis_index(name) for name in ("groups", "sector", "term"))
    half = psi_ref.shape[0] // 2
    terms = left_ref.shape[0]
    mine = pl.ds(core * half, half)
    barrier = pltpu.get_barrier_semaphore()
    sibling = (group, sector, 1 - core)
    there = [has_source(sector, sectors, step) for step in STEPS]
    wanted = [has_source(sector, sectors, -step) for step in STEPS]
    count = jnp.int32(1)
    pl.semaphore_signal(barrier, inc=1, device_id=sibling, device_id_type=MESH)
    for slot, step in enumerate(STEPS):
        count = count + there[slot].astype(jnp.int32)

        @pl.when(there[slot])
        def _():
            pl.semaphore_signal(barrier, inc=1, device_id=(group, sector + step, core), device_id_type=MESH)

    pl.semaphore_wait(barrier, count)

    def outgoing(slot):
        return pltpu.make_async_remote_copy(
            src_ref=psi_ref.at[mine],
            dst_ref=got_ref.at[slot, mine],
            send_sem=send_sem.at[slot],
            recv_sem=recv_sem.at[slot],
            device_id=(group, sector - STEPS[slot], core),
            device_id_type=MESH,
        )

    def passing(slot):
        return pltpu.make_async_remote_copy(
            src_ref=got_ref.at[slot, mine],
            dst_ref=got_ref.at[slot, mine],
            send_sem=pass_sem.at[slot],
            recv_sem=got_sem.at[slot],
            device_id=sibling,
            device_id_type=MESH,
        )

    def arrive(slot):
        @pl.when(there[slot])
        def _():
            outgoing(slot).wait_recv()
            passing(slot).start()

    def load(slot):
        @pl.when(there[slot])
        def _():
            passing(slot).wait()
            copy = pltpu.make_async_copy(got_ref.at[slot], tiles.at[slot + 1], local_sem.at[3])
            copy.start()
            copy.wait()

    for slot in range(len(STEPS)):
        pl.when(wanted[slot])(lambda slot=slot: outgoing(slot).start())
    copies = [
        pltpu.make_async_copy(psi_ref, tiles.at[0], local_sem.at[0]),
        pltpu.make_async_copy(left_ref, lefts, local_sem.at[1]),
        pltpu.make_async_copy(right_ref, rights, local_sem.at[2]),
    ]
    for copy in copies:
        copy.start()

    def note(index, state):
        fresh = []
        for kind, (found, slots) in enumerate(state):
            match = class_ref[index] == kind
            slots = tuple(jnp.where(match & (found == n), index, slot) for n, slot in enumerate(slots))
            fresh.append((found + match.astype(jnp.int32), slots))
        return tuple(fresh)

    zero = jnp.int32(0)
    state = lax.fori_loop(0, terms, note, tuple((zero, (zero,) * FRONT_SLOTS) for _ in range(FRONT_KINDS)))
    for kind, (found, slots) in enumerate(state):
        for n, slot in enumerate(slots):
            plan[0, kind * FRONT_SLOTS + n] = slot
            plan[1, kind * FRONT_SLOTS + n] = (n < found).astype(jnp.int32)
    acc[...] = jnp.zeros_like(acc)
    for copy in copies:
        copy.wait()

    @pl.loop(0, FRONT_KINDS)
    def _(phase):
        @pl.when(phase == 1)
        def _():
            arrive(0)
            arrive(1)
            load(0)

        @pl.when(phase == 2)
        def _():
            load(1)

        live = (phase == 0) | ((phase == 1) & there[0]) | ((phase == 2) & there[1])

        @pl.when(live)
        def _():
            @pl.loop(0, FRONT_SLOTS // 2)
            def _(pair):
                spot = [phase * FRONT_SLOTS + 2 * pair + t for t in range(2)]
                term = [plan[0, n] for n in spot]
                add_pair(
                    [lambda s: tiles[phase, pl.ds(s, 2)]] * 2,
                    [rights[i] for i in term],
                    [mpo_ref[i] for i in term],
                    [lefts[i] for i in term],
                    [plan[1, n].astype(jnp.float32) for n in spot],
                    held, mixed, acc,
                )

    for slot in (2, 3):
        arrive(slot)
    for slot in range(len(STEPS)):
        if slot >= 2:
            pl.when(there[slot])(lambda slot=slot: passing(slot).wait())
        pl.when(wanted[slot])(lambda slot=slot: outgoing(slot).wait_send())


SMEM_SPEC = pl.BlockSpec(memory_space=pltpu.SMEM)
VMEM_SPEC = pl.BlockSpec(memory_space=pltpu.VMEM)
ANY_SPEC = pl.BlockSpec(memory_space=pl.ANY)


def front(term_class, psi, left, right, mpo, sectors):
    states, rows, width = psi.shape
    slots = len(STEPS)
    return pl.pallas_call(
        functools.partial(front_kernel, sectors),
        out_shape=(
            jax.ShapeDtypeStruct((slots, *psi.shape), psi.dtype),
            jax.ShapeDtypeStruct(psi.shape, jnp.float32),
        ),
        in_specs=[SMEM_SPEC, ANY_SPEC, ANY_SPEC, ANY_SPEC, VMEM_SPEC],
        out_specs=(ANY_SPEC, VMEM_SPEC),
        scratch_shapes=[
            pltpu.VMEM((FRONT_KINDS, states, rows, width), jnp.bfloat16),
            pltpu.VMEM(left.shape, jnp.bfloat16),
            pltpu.VMEM(right.shape, jnp.bfloat16),
            pltpu.VMEM((states, rows, 2 * width), jnp.bfloat16),
            pltpu.VMEM((2, states, rows, width), jnp.bfloat16),
            pltpu.SMEM((2, FRONT_KINDS * FRONT_SLOTS), jnp.int32),
        ] + [pltpu.SemaphoreType.DMA((slots,))] * 5,
        compiler_params=pltpu.CompilerParams(collective_id=0, has_side_effects=True, vmem_limit_bytes=VMEM_LIMIT),
        name="front",
    )(term_class, psi, left, right, mpo)


def rest_kernel(sectors, class_ref, psi_ref, got_ref, left_ref, right_ref, mpo_ref, total_ref, own_ref, sent_ref,
                tiles, lefts, rights, acc, held, mixed, plan, tile_sem, left_sem, right_sem, acc_sem):
    sector, core = lax.axis_index("sector"), lax.axis_index("term")
    terms = left_ref.shape[0]
    states = acc.shape[0]
    start = pltpu.make_async_copy(total_ref, acc, acc_sem)
    start.start()
    used = jnp.int32(0)
    need = []
    for kind in range(len(STEPS) + 1):
        there = jnp.bool_(True) if kind == 0 else has_source(sector, sectors, STEPS[kind - 1])
        skip = FRONT_SLOTS if kind < FRONT_KINDS else 0
        before = used

        def note(index, state, kind=kind, there=there, skip=skip):
            used, found = state
            match = (class_ref[index] == kind) & there
            plan[0, used] = index
            plan[1, used] = kind
            take = match & (found >= skip)
            return used + take.astype(jnp.int32), found + match.astype(jnp.int32)

        used, found = lax.fori_loop(0, terms, note, (used, jnp.int32(0)), unroll=True)
        need.append(used > before)
    plan[0, used] = 0
    plan[1, used] = plan[1, jnp.maximum(used - 1, 0)]
    padded = 2 * ((used + 1) // 2)

    def tile_copy(kind):
        source = psi_ref if kind == 0 else got_ref.at[kind - 1]
        return pltpu.make_async_copy(source, tiles.at[kind], tile_sem.at[kind])

    def side_copies(n):
        term = plan[0, n]
        return (pltpu.make_async_copy(left_ref.at[term], lefts.at[n], left_sem.at[n]),
                pltpu.make_async_copy(right_ref.at[term], rights.at[n], right_sem.at[n]))

    for kind, wanted in enumerate(need):
        pl.when(wanted)(lambda kind=kind: tile_copy(kind).start())

    @pl.loop(0, padded)
    def _(n):
        for copy in side_copies(n):
            copy.start()

    start.wait()
    for kind, wanted in enumerate(need):
        pl.when(wanted)(lambda kind=kind: tile_copy(kind).wait())

    @pl.loop(0, padded // 2)
    def _(pair):
        spot = [2 * pair + t for t in range(2)]
        for n in spot:
            for copy in side_copies(n):
                copy.wait()
        kind = [plan[1, n] for n in spot]
        add_pair(
            [lambda s, k=k: tiles[k, pl.ds(s, 2)] for k in kind],
            [rights[n] for n in spot],
            [mpo_ref[plan[0, n]] for n in spot],
            [lefts[n] for n in spot],
            [(n < used).astype(jnp.float32) for n in spot],
            held, mixed, acc,
        )

    half = states // 2
    own_ref[...] = acc[pl.ds(core * half, half)]
    sent_ref[...] = acc[pl.ds((1 - core) * half, half)].astype(sent_ref.dtype)


def rest(term_class, psi, got, left, right, mpo, total, sectors):
    states, rows, width = psi.shape
    terms = left.shape[0]
    half = (states // 2, rows, width)
    return pl.pallas_call(
        functools.partial(rest_kernel, sectors),
        out_shape=(jax.ShapeDtypeStruct(half, jnp.float32), jax.ShapeDtypeStruct(half, jnp.bfloat16)),
        in_specs=[SMEM_SPEC, ANY_SPEC, ANY_SPEC, ANY_SPEC, ANY_SPEC, VMEM_SPEC, ANY_SPEC],
        out_specs=(VMEM_SPEC, VMEM_SPEC),
        scratch_shapes=[
            pltpu.VMEM((len(STEPS) + 1, states, rows, width), jnp.bfloat16),
            pltpu.VMEM((terms + 1, *left.shape[1:]), jnp.bfloat16),
            pltpu.VMEM((terms + 1, *right.shape[1:]), jnp.bfloat16),
            pltpu.VMEM((states, rows, width), jnp.float32),
            pltpu.VMEM((states, rows, 2 * width), jnp.bfloat16),
            pltpu.VMEM((2, states, rows, width), jnp.bfloat16),
            pltpu.SMEM((2, terms + 2), jnp.int32),
            pltpu.SemaphoreType.DMA((len(STEPS) + 1,)),
            pltpu.SemaphoreType.DMA((terms + 1,)),
            pltpu.SemaphoreType.DMA((terms + 1,)),
            pltpu.SemaphoreType.DMA(()),
        ],
        compiler_params=pltpu.CompilerParams(vmem_limit_bytes=VMEM_LIMIT),
        name="rest",
    )(term_class, psi, got, left, right, mpo, total)


def swap_kernel(sent_ref, inbox_ref, sems):
    group, sector, core = (lax.axis_index(name) for name in ("groups", "sector", "term"))
    sibling = (group, sector, 1 - core)
    barrier = pltpu.get_barrier_semaphore()
    pl.semaphore_signal(barrier, inc=1, device_id=sibling, device_id_type=MESH)
    pl.semaphore_wait(barrier, 1)
    copy = pltpu.make_async_remote_copy(
        src_ref=sent_ref, dst_ref=inbox_ref, send_sem=sems.at[0], recv_sem=sems.at[1],
        device_id=sibling, device_id_type=MESH,
    )
    copy.start()
    copy.wait()


def swapped(sent):
    return pl.pallas_call(
        swap_kernel,
        out_shape=jax.ShapeDtypeStruct(sent.shape, sent.dtype),
        in_specs=[ANY_SPEC],
        out_specs=ANY_SPEC,
        scratch_shapes=[pltpu.SemaphoreType.DMA((2,))],
        compiler_params=pltpu.CompilerParams(collective_id=1, has_side_effects=True, vmem_limit_bytes=VMEM_LIMIT),
        name="swap",
    )(sent)


def shards(psi_tiles, env_left, env_right, mpo_local, term_class):
    sectors = lax.axis_size("sector")
    psi, left, right = psi_tiles[0], env_left[0], env_right[0]
    got, total = front(term_class, psi, left, right, mpo_local, sectors)
    own, sent = rest(term_class, psi, got, left, right, mpo_local, total, sectors)
    return (own + swapped(sent).astype(jnp.float32)).astype(jnp.bfloat16)[None]


def solution(mesh):
    placed = (
        P(("groups", "sector"), None, None, None),
        P(("groups", "sector"), "term", None, None),
        P(("groups", "sector"), "term", None, None),
        P(("groups", "term"), None, None),
        P(("groups", "term")),
    )
    return jax.shard_map(
        shards,
        mesh=mesh,
        in_specs=placed,
        out_specs=P(("groups", "sector"), "term", None, None),
        check_vma=False,
    )
```

time: 283 us -> 65.7 us (0.23)
  the two profiles are of different devices: /device:TPU:9 before, /device:TPU:7 now
where the time goes in v2:
time: 65.7 us; the launch traced here: 65.4 us
  Pallas kernels  61.5 us (94%)
  other arithmetic  2.26 us (3%)
  local copies, waits for them, and re-layouts  1.64 us (2%)
    pallas_call x1, Pallas kernels, front(): pl.pallas_call(functools.partial(front_kernel, sectors), out_shape=(jax.S...  48.1 us
    pallas_call x1, Pallas kernels, rest(): pl.pallas_call(functools.partial(rest_kernel, sectors), out_shape=(jax.Sh...  11.1 us
    pallas_call x1, Pallas kernels, swapped(): pl.pallas_call(swap_kernel, out_shape=jax.ShapeDtypeStruct(sent.shape, se...  2.3 us
    broadcast_in_dim x1, other arithmetic, shards(): return (own + swapped(sent).astype(jnp.float32)).astype(jnp.bfloat16)[None]  2.26 us
    unnamed x1, local copies, waits for them, and re-layouts  1.64 us

profile of v2, /device:TPU:7, one launch (start us, length us, event | category | flops | bytes accessed | tf_op | source)
XLA Modules:
  0.0 65.4 jit_solution(2257788943209676345)
XLA Ops:
  0.0 1.6 %copy.6.mpo_ref = bf16[17,16,16]{2,1,0:T(8,128)(2,1)} copy(bf16[17,16,16]{0,2,1:T(8,128)(2,1)} %param.8) | data formatting | bytes 17408 | tf_op args[3]
  1.6 48.1 %front.1 = (bf16[4,16,256,128]{3,2,1,0:T(8,128)(2,1)}, f32[16,256,128]{2,1,0:T(8,128)}) custom-call(s32[17]{0:T(128)} %class_ref.3, bf16[16,256,128]{2,1,0:T(8,128)(2,1)} %bitcast.7, bf16[17,256,256]{2,1,0:T(8,128)(2,1)} %bitcast.5, bf16[17,128,128]{2,1,0:T(8,128)(2,1)} %bitcast.9, bf16[17,16,16]{2,1,0:T(8,128)(2,1)} %copy.6.mpo_ref), custom_call_target="tpu_custom_call" | custom-call | tf_op jit(solution)/shard_map/front/pallas_call | solution.py:197
  49.8 11.1 %rest.1 = (f32[8,256,128]{2,1,0:T(8,128)}, bf16[8,256,128]{2,1,0:T(8,128)(2,1)}) custom-call(s32[17]{0:T(128)} %class_ref.3, bf16[16,256,128]{2,1,0:T(8,128)(2,1)} %bitcast.8, bf16[4,16,256,128]{3,2,1,0:T(8,128)(2,1)} %get-tuple-element.9.got_ref, bf16[17,256,256]{2,1,0:T(8,128)(2,1)} %bitcast.6, bf16[17,128,128]{2,1,0:T(8,128)(2,1)} %bitcast.10, ...), custom_call_target="tpu_custom_call" | custom-call | tf_op jit(solution)/shard_map/rest/pallas_call | solution.py:292
  60.8 2.3 %swap.1 = bf16[8,256,128]{2,1,0:T(8,128)(2,1)} custom-call(bf16[8,256,128]{2,1,0:T(8,128)(2,1)} %get-tuple-element.12.sent_ref), custom_call_target="tpu_custom_call" | custom-call | tf_op jit(solution)/shard_map/swap/pallas_call | solution.py:330
  63.1 2.3 %fusion = bf16[1,8,256,128]{3,2,1,0:T(8,128)(2,1)} fusion(f32[8,256,128]{2,1,0:T(8,128)} %get-tuple-element.11, bf16[8,256,128]{2,1,0:T(8,128)(2,1)} %swap.1), kind=kLoop, calls=%fused_computation.1 | loop fusion | flops 786432 | bytes 2097152 | tf_op jit(solution)/shard_map/broadcast_in_dim | solution.py:346

commit v3 on v2

--- a/solution.py
+++ b/solution.py
@@ -10,7 +10,7 @@
 GRID = 4
 MESH = pl.DeviceIdType.MESH
 STEPS = (-1, 1, -GRID, GRID)
-FRONT_KINDS, FRONT_SLOTS = 3, 6
+FRONT_KINDS, FRONT_SLOTS = 2, 8
 VMEM_LIMIT = 56 * 1024 * 1024
 
 
@@ -74,28 +74,53 @@
     mine = pl.ds(core * half, half)
     barrier = pltpu.get_barrier_semaphore()
     sibling = (group, sector, 1 - core)
+    assert sectors % 2 == 0
     there = [has_source(sector, sectors, step) for step in STEPS]
-    wanted = [has_source(sector, sectors, -step) for step in STEPS]
-    count = jnp.int32(1)
-    pl.semaphore_signal(barrier, inc=1, device_id=sibling, device_id_type=MESH)
-    for slot, step in enumerate(STEPS):
-        count = count + there[slot].astype(jnp.int32)
-
-        @pl.when(there[slot])
-        def _():
-            pl.semaphore_signal(barrier, inc=1, device_id=(group, sector + step, core), device_id_type=MESH)
-
-    pl.semaphore_wait(barrier, count)
-
-    def outgoing(slot):
+    odd = lax.rem(sector, 2) == 1
+    even = jnp.logical_not(odd)
+    above, below = sector + 2 < sectors, sector >= 2
+    partner = jnp.where(odd, sector - 1, sector + 1)
+    near = jnp.where(odd, 0, 1)
+    near_there = (odd & there[0]) | (even & there[1])
+    up_out = above & ((sector + 4 < sectors) | (odd & there[1]))
+    up_in = below & (above | (odd & has_source(sector - 2, sectors, 1)))
+    down_out = below & ((sector >= 4) | (even & there[0]))
+    down_in = above & (below | (even & has_source(sector + 2, sectors, -1)))
+    across_0 = odd & below & has_source(sector - 1, sectors, -1)
+    across_1 = even & above & has_source(sector + 1, sectors, 1)
+    through = above & below
+
+    def greet(target):
+        pl.semaphore_signal(barrier, inc=1, device_id=target, device_id_type=MESH)
+
+    greet(sibling)
+    greet((group, partner, core))
+    pl.when(above)(lambda: greet((group, sector + 2, core)))
+    pl.when(below)(lambda: greet((group, sector - 2, core)))
+    pl.semaphore_wait(barrier, 2 + above.astype(jnp.int32) + below.astype(jnp.int32))
+
+    def send(source, slot, target):
         return pltpu.make_async_remote_copy(
-            src_ref=psi_ref.at[mine],
+            src_ref=source,
             dst_ref=got_ref.at[slot, mine],
             send_sem=send_sem.at[slot],
             recv_sem=recv_sem.at[slot],
-            device_id=(group, sector - STEPS[slot], core),
+            device_id=(group, target, core),
             device_id_type=MESH,
         )
+
+    tile, lower, upper = psi_ref.at[mine], got_ref.at[4, mine], got_ref.at[5, mine]
+    first = (
+        (up_out, lambda: send(tile, 4, sector + 2)),
+        (down_out, lambda: send(tile, 5, sector - 2)),
+        (near_there, lambda: send(tile, 1 - near, partner)),
+    )
+    second = (
+        (across_0, lambda: send(lower, 0, partner)),
+        (through, lambda: send(lower, 2, sector + 2)),
+        (across_1, lambda: send(upper, 1, partner)),
+        (through, lambda: send(upper, 3, sector - 2)),
+    )
 
     def passing(slot):
         return pltpu.make_async_remote_copy(
@@ -108,21 +133,11 @@
         )
 
     def arrive(slot):
-        @pl.when(there[slot])
-        def _():
-            outgoing(slot).wait_recv()
-            passing(slot).start()
-
-    def load(slot):
-        @pl.when(there[slot])
-        def _():
-            passing(slot).wait()
-            copy = pltpu.make_async_copy(got_ref.at[slot], tiles.at[slot + 1], local_sem.at[3])
-            copy.start()
-            copy.wait()
-
-    for slot in range(len(STEPS)):
-        pl.when(wanted[slot])(lambda slot=slot: outgoing(slot).start())
+        send(tile, slot, partner).wait_recv()
+        passing(slot).start()
+
+    for live, copy in first:
+        pl.when(live)(lambda copy=copy: copy().start())
     copies = [
         pltpu.make_async_copy(psi_ref, tiles.at[0], local_sem.at[0]),
         pltpu.make_async_copy(left_ref, lefts, local_sem.at[1]),
@@ -134,7 +149,7 @@
     def note(index, state):
         fresh = []
         for kind, (found, slots) in enumerate(state):
-            match = class_ref[index] == kind
+            match = class_ref[index] == (0 if kind == 0 else near + 1)
             slots = tuple(jnp.where(match & (found == n), index, slot) for n, slot in enumerate(slots))
             fresh.append((found + match.astype(jnp.int32), slots))
         return tuple(fresh)
@@ -153,15 +168,27 @@
     def _(phase):
         @pl.when(phase == 1)
         def _():
-            arrive(0)
-            arrive(1)
-            load(0)
-
-        @pl.when(phase == 2)
-        def _():
-            load(1)
-
-        live = (phase == 0) | ((phase == 1) & there[0]) | ((phase == 2) & there[1])
+            @pl.when(up_in)
+            def _():
+                send(tile, 4, partner).wait_recv()
+                for live, copy in second[:2]:
+                    pl.when(live)(lambda copy=copy: copy().start())
+
+            @pl.when(down_in)
+            def _():
+                send(tile, 5, partner).wait_recv()
+                for live, copy in second[2:]:
+                    pl.when(live)(lambda copy=copy: copy().start())
+
+            @pl.when(near_there)
+            def _():
+                arrive(near)
+                passing(near).wait()
+                copy = pltpu.make_async_copy(got_ref.at[near], tiles.at[1], local_sem.at[3])
+                copy.start()
+                copy.wait()
+
+        live = (phase == 0) | near_there
 
         @pl.when(live)
         def _():
@@ -178,12 +205,13 @@
                     held, mixed, acc,
                 )
 
-    for slot in (2, 3):
-        arrive(slot)
-    for slot in range(len(STEPS)):
-        if slot >= 2:
-            pl.when(there[slot])(lambda slot=slot: passing(slot).wait())
-        pl.when(wanted[slot])(lambda slot=slot: outgoing(slot).wait_send())
+    late = ((odd & there[1]) | (even & there[0]), 1 - near), (there[2], 2), (there[3], 3)
+    for live, slot in late:
+        pl.when(live)(lambda slot=slot: arrive(slot))
+    for live, slot in late:
+        pl.when(live)(lambda slot=slot: passing(slot).wait())
+    for live, copy in first + second:
+        pl.when(live)(lambda copy=copy: copy().wait_send())
 
 
 SMEM_SPEC = pl.BlockSpec(memory_space=pltpu.SMEM)
@@ -197,7 +225,7 @@
     return pl.pallas_call(
         functools.partial(front_kernel, sectors),
         out_shape=(
-            jax.ShapeDtypeStruct((slots, *psi.shape), psi.dtype),
+            jax.ShapeDtypeStruct((slots + 2, *psi.shape), psi.dtype),
             jax.ShapeDtypeStruct(psi.shape, jnp.float32),
         ),
         in_specs=[SMEM_SPEC, ANY_SPEC, ANY_SPEC, ANY_SPEC, VMEM_SPEC],
@@ -209,7 +237,7 @@
             pltpu.VMEM((states, rows, 2 * width), jnp.bfloat16),
             pltpu.VMEM((2, states, rows, width), jnp.bfloat16),
             pltpu.SMEM((2, FRONT_KINDS * FRONT_SLOTS), jnp.int32),
-        ] + [pltpu.SemaphoreType.DMA((slots,))] * 5,
+        ] + [pltpu.SemaphoreType.DMA((slots + 2,))] * 5,
         compiler_params=pltpu.CompilerParams(collective_id=0, has_side_effects=True, vmem_limit_bytes=VMEM_LIMIT),
         name="front",
     )(term_class, psi, left, right, mpo)
@@ -222,11 +250,12 @@
     states = acc.shape[0]
     start = pltpu.make_async_copy(total_ref, acc, acc_sem)
     start.start()
+    near = 2 - lax.rem(sector, 2)
     used = jnp.int32(0)
     need = []
     for kind in range(len(STEPS) + 1):
         there = jnp.bool_(True) if kind == 0 else has_source(sector, sectors, STEPS[kind - 1])
-        skip = FRONT_SLOTS if kind < FRONT_KINDS else 0
+        skip = FRONT_SLOTS if kind == 0 else jnp.where(near == kind, FRONT_SLOTS, 0)
         before = used
 
         def note(index, state, kind=kind, there=there, skip=skip):

time: 65.7 us -> 54.7 us (0.83)
  the two profiles are of different devices: /device:TPU:7 before, /device:TPU:9 now
where the time goes in v3:
time: 54.7 us; the launch traced here: 54.4 us
  Pallas kernels  50.5 us (92%)
  other arithmetic  2.26 us (4%)
  local copies, waits for them, and re-layouts  1.63 us (3%)
    pallas_call x1, Pallas kernels, front(): pl.pallas_call(functools.partial(front_kernel, sectors), out_shape=(jax.S...  33 us
    pallas_call x1, Pallas kernels, rest(): pl.pallas_call(functools.partial(rest_kernel, sectors), out_shape=(jax.Sh...  11.3 us
    pallas_call x1, Pallas kernels, swapped(): pl.pallas_call(swap_kernel, out_shape=jax.ShapeDtypeStruct(sent.shape, se...  6.25 us
    broadcast_in_dim x1, other arithmetic, shards(): return (own + swapped(sent).astype(jnp.float32)).astype(jnp.bfloat16)[None]  2.26 us
    unnamed x1, local copies, waits for them, and re-layouts  1.63 us

profile of v3, /device:TPU:9, one launch (start us, length us, event | category | flops | bytes accessed | tf_op | source)
XLA Modules:
  0.0 54.4 jit_solution(15101466128519521838)
XLA Ops:
  0.0 1.6 %copy.6.mpo_ref = bf16[17,16,16]{2,1,0:T(8,128)(2,1)} copy(bf16[17,16,16]{0,2,1:T(8,128)(2,1)} %param.8) | data formatting | bytes 17408 | tf_op args[3]
  1.6 33.0 %front.1 = (bf16[6,16,256,128]{3,2,1,0:T(8,128)(2,1)}, f32[16,256,128]{2,1,0:T(8,128)}) custom-call(s32[17]{0:T(128)} %class_ref.3, bf16[16,256,128]{2,1,0:T(8,128)(2,1)} %bitcast.7, bf16[17,256,256]{2,1,0:T(8,128)(2,1)} %bitcast.5, bf16[17,128,128]{2,1,0:T(8,128)(2,1)} %bitcast.9, bf16[17,16,16]{2,1,0:T(8,128)(2,1)} %copy.6.mpo_ref), custom_call_target="tpu_custom_call" | custom-call | tf_op jit(solution)/shard_map/front/pallas_call | solution.py:225
  34.6 11.3 %rest.1 = (f32[8,256,128]{2,1,0:T(8,128)}, bf16[8,256,128]{2,1,0:T(8,128)(2,1)}) custom-call(s32[17]{0:T(128)} %class_ref.3, bf16[16,256,128]{2,1,0:T(8,128)(2,1)} %bitcast.8, bf16[6,16,256,128]{3,2,1,0:T(8,128)(2,1)} %get-tuple-element.9.got_ref, bf16[17,256,256]{2,1,0:T(8,128)(2,1)} %bitcast.6, bf16[17,128,128]{2,1,0:T(8,128)(2,1)} %bitcast.10, ...), custom_call_target="tpu_custom_call" | custom-call | tf_op jit(solution)/shard_map/rest/pallas_call | solution.py:321
  45.9 6.2 %swap.1 = bf16[8,256,128]{2,1,0:T(8,128)(2,1)} custom-call(bf16[8,256,128]{2,1,0:T(8,128)(2,1)} %get-tuple-element.12.sent_ref), custom_call_target="tpu_custom_call" | custom-call | tf_op jit(solution)/shard_map/swap/pallas_call | solution.py:359
  52.1 2.3 %fusion = bf16[1,8,256,128]{3,2,1,0:T(8,128)(2,1)} fusion(f32[8,256,128]{2,1,0:T(8,128)} %get-tuple-element.11, bf16[8,256,128]{2,1,0:T(8,128)(2,1)} %swap.1), kind=kLoop, calls=%fused_computation.1 | loop fusion | flops 786432 | bytes 2097152 | tf_op jit(solution)/shard_map/broadcast_in_dim | solution.py:375

commit v4 on v3

--- a/solution.py
+++ b/solution.py
@@ -25,24 +25,27 @@
     return sector + step < sectors
 
 
-def add_pair(xs, rights, mpos, lefts, scales, held, mixed, acc):
+def add_pair(xs, rights, mpo_ref, terms, lefts, scales, held, mixed, acc):
     states, rows, width = acc.shape
     step = 16
     wide = states * step
     index = lambda axis: lax.broadcasted_iota(jnp.int32, (wide, wide), axis)
     same = lax.rem(index(0), step) == lax.rem(index(1), step)
-    spread = (lax.broadcasted_iota(jnp.int32, (wide, states), 0) // step
-              == lax.broadcasted_iota(jnp.int32, (wide, states), 1)).astype(jnp.bfloat16)
-    spread_t = (lax.broadcasted_iota(jnp.int32, (states, wide), 1) // step
-                == lax.broadcasted_iota(jnp.int32, (states, wide), 0)).astype(jnp.bfloat16)
+    entry = lambda axis: lax.broadcasted_iota(jnp.int32, (states * states, wide), axis)
+    column = lax.rem(entry(0), states) == entry(1) // step
+    spread = (lax.broadcasted_iota(jnp.int32, (wide, states * states), 0) // step
+              == lax.broadcasted_iota(jnp.int32, (wide, states * states), 1) // states).astype(jnp.bfloat16)
+    flat = mpo_ref[...].reshape(states * states, mpo_ref.shape[2]).astype(jnp.float32)
+    number = lax.broadcasted_iota(jnp.int32, flat.shape, 1)
 
     def dot(a, b):
         return jnp.dot(a, b, preferred_element_type=jnp.float32)
 
     krons = []
-    for mpo, scale in zip(mpos, scales):
-        tall = dot(spread, mpo).astype(jnp.bfloat16)
-        krons.append(jnp.where(same, dot(tall, spread_t) * scale, 0.0).astype(jnp.bfloat16))
+    for term, scale in zip(terms, scales):
+        values = jnp.sum(jnp.where(number == term, flat, 0.0), 1, keepdims=True) * scale
+        wide_rows = jnp.where(column, values, 0.0).astype(jnp.bfloat16)
+        krons.append(jnp.where(same, dot(spread, wide_rows), 0.0).astype(jnp.bfloat16))
     zero = jnp.zeros((width, width), jnp.bfloat16)
     right = jnp.concatenate(
         [jnp.concatenate([rights[0], zero], 1), jnp.concatenate([zero, rights[1]], 1)], 0
@@ -199,7 +202,7 @@
                 add_pair(
                     [lambda s: tiles[phase, pl.ds(s, 2)]] * 2,
                     [rights[i] for i in term],
-                    [mpo_ref[i] for i in term],
+                    mpo_ref, term,
                     [lefts[i] for i in term],
                     [plan[1, n].astype(jnp.float32) for n in spot],
                     held, mixed, acc,
@@ -303,7 +306,7 @@
         add_pair(
             [lambda s, k=k: tiles[k, pl.ds(s, 2)] for k in kind],
             [rights[n] for n in spot],
-            [mpo_ref[plan[0, n]] for n in spot],
+            mpo_ref, [plan[0, n] for n in spot],
             [lefts[n] for n in spot],
             [(n < used).astype(jnp.float32) for n in spot],
             held, mixed, acc,
@@ -370,8 +373,9 @@
 def shards(psi_tiles, env_left, env_right, mpo_local, term_class):
     sectors = lax.axis_size("sector")
     psi, left, right = psi_tiles[0], env_left[0], env_right[0]
-    got, total = front(term_class, psi, left, right, mpo_local, sectors)
-    own, sent = rest(term_class, psi, got, left, right, mpo_local, total, sectors)
+    mpo = jnp.transpose(mpo_local, (1, 2, 0))
+    got, total = front(term_class, psi, left, right, mpo, sectors)
+    own, sent = rest(term_class, psi, got, left, right, mpo, total, sectors)
     return (own + swapped(sent).astype(jnp.float32)).astype(jnp.bfloat16)[None]
 
 

time: 54.7 us -> 54.1 us (0.989)
  the two profiles are of different devices: /device:TPU:9 before, /device:TPU:3 now
where the time goes in v4:
time: 54.1 us; the launch traced here: 53.2 us
  Pallas kernels  50.9 us (94%)
  other arithmetic  2.26 us (4%)
    pallas_call x1, Pallas kernels, front(): pl.pallas_call(functools.partial(front_kernel, sectors), out_shape=(jax.S...  33 us
    pallas_call x1, Pallas kernels, rest(): pl.pallas_call(functools.partial(rest_kernel, sectors), out_shape=(jax.Sh...  15.6 us
    pallas_call x1, Pallas kernels, swapped(): pl.pallas_call(swap_kernel, out_shape=jax.ShapeDtypeStruct(sent.shape, se...  2.3 us
    broadcast_in_dim x1, other arithmetic, shards(): return (own + swapped(sent).astype(jnp.float32)).astype(jnp.bfloat16)[None]  2.26 us

profile of v4, /device:TPU:3, one launch (start us, length us, event | category | flops | bytes accessed | tf_op | source)
XLA Modules:
  0.0 53.2 jit_solution(4728735394151770894)
XLA Ops:
  0.0 33.0 %front.1 = (bf16[6,16,256,128]{3,2,1,0:T(8,128)(2,1)}, f32[16,256,128]{2,1,0:T(8,128)}) custom-call(s32[17]{0:T(128)} %class_ref.3, bf16[16,256,128]{2,1,0:T(8,128)(2,1)} %bitcast.8, bf16[17,256,256]{2,1,0:T(8,128)(2,1)} %bitcast.6, bf16[17,128,128]{2,1,0:T(8,128)(2,1)} %bitcast.10, bf16[16,16,17]{2,1,0:T(8,128)(2,1)} %bitcast.12), custom_call_target="tpu_custom_call" | custom-call | tf_op jit(solution)/shard_map/front/pallas_call | solution.py:228
  33.0 15.6 %rest.1 = (f32[8,256,128]{2,1,0:T(8,128)}, bf16[8,256,128]{2,1,0:T(8,128)(2,1)}) custom-call(s32[17]{0:T(128)} %class_ref.3, bf16[16,256,128]{2,1,0:T(8,128)(2,1)} %bitcast.9, bf16[6,16,256,128]{3,2,1,0:T(8,128)(2,1)} %get-tuple-element.9.got_ref, bf16[17,256,256]{2,1,0:T(8,128)(2,1)} %bitcast.7, bf16[17,128,128]{2,1,0:T(8,128)(2,1)} %bitcast.11, ...), custom_call_target="tpu_custom_call" | custom-call | tf_op jit(solution)/shard_map/rest/pallas_call | solution.py:324
  48.6 2.3 %swap.1 = bf16[8,256,128]{2,1,0:T(8,128)(2,1)} custom-call(bf16[8,256,128]{2,1,0:T(8,128)(2,1)} %get-tuple-element.12.sent_ref), custom_call_target="tpu_custom_call" | custom-call | tf_op jit(solution)/shard_map/swap/pallas_call | solution.py:362
  50.9 2.3 %fusion = bf16[1,8,256,128]{3,2,1,0:T(8,128)(2,1)} fusion(f32[8,256,128]{2,1,0:T(8,128)} %get-tuple-element.11, bf16[8,256,128]{2,1,0:T(8,128)(2,1)} %swap.1), kind=kLoop, calls=%fused_computation.1 | loop fusion | flops 786432 | bytes 2097152 | tf_op jit(solution)/shard_map/broadcast_in_dim | solution.py:379

commit v5 on v4

--- a/solution.py
+++ b/solution.py
@@ -25,7 +25,7 @@
     return sector + step < sectors
 
 
-def add_pair(xs, rights, mpo_ref, terms, lefts, scales, held, mixed, acc):
+def add_pair(xs, rights, mpo_ref, terms, lefts, scales, held, mixed, acc, before_sum=lambda: None):
     states, rows, width = acc.shape
     step = 16
     wide = states * step
@@ -61,6 +61,7 @@
             out = dot(krons[t], jnp.concatenate(part, 1)).astype(jnp.bfloat16)
             for n, o in enumerate((0, step)):
                 mixed[t, :, pl.ds(r + o, step), :] = out[:, n * width:(n + 1) * width].reshape(states, step, width)
+    before_sum()
     left = jnp.concatenate(lefts, 1)
     for s in range(0, states, 2):
         part = [jnp.concatenate([mixed[t, s], mixed[t, s + 1]], 1) for t in range(2)]
@@ -252,7 +253,6 @@
     terms = left_ref.shape[0]
     states = acc.shape[0]
     start = pltpu.make_async_copy(total_ref, acc, acc_sem)
-    start.start()
     near = 2 - lax.rem(sector, 2)
     used = jnp.int32(0)
     need = []
@@ -292,24 +292,28 @@
         for copy in side_copies(n):
             copy.start()
 
-    start.wait()
-    for kind, wanted in enumerate(need):
-        pl.when(wanted)(lambda kind=kind: tile_copy(kind).wait())
+    start.start()
+    pl.when(padded == 0)(lambda: start.wait())
 
     @pl.loop(0, padded // 2)
     def _(pair):
         spot = [2 * pair + t for t in range(2)]
-        for n in spot:
+        kind = [plan[1, n] for n in spot]
+        for n, k in zip(spot, kind):
             for copy in side_copies(n):
                 copy.wait()
-        kind = [plan[1, n] for n in spot]
+
+            @pl.when((n == 0) | (k != plan[1, jnp.maximum(n - 1, 0)]))
+            def _():
+                pltpu.make_async_copy(psi_ref, tiles.at[k], tile_sem.at[k]).wait()
+
         add_pair(
             [lambda s, k=k: tiles[k, pl.ds(s, 2)] for k in kind],
             [rights[n] for n in spot],
             mpo_ref, [plan[0, n] for n in spot],
             [lefts[n] for n in spot],
             [(n < used).astype(jnp.float32) for n in spot],
-            held, mixed, acc,
+            held, mixed, acc, lambda: pl.when(pair == 0)(lambda: start.wait()),
         )
 
     half = states // 2

time: 54.1 us -> 55.8 us (1.031)
  the two profiles are of different devices: /device:TPU:3 before, /device:TPU:9 now
where the time goes in v5:
time: 55.8 us; the launch traced here: 55.5 us
  Pallas kernels  53.2 us (95%)
  other arithmetic  2.26 us (4%)
    pallas_call x1, Pallas kernels, front(): pl.pallas_call(functools.partial(front_kernel, sectors), out_shape=(jax.S...  32.9 us
    pallas_call x1, Pallas kernels, rest(): pl.pallas_call(functools.partial(rest_kernel, sectors), out_shape=(jax.Sh...  11.2 us
    pallas_call x1, Pallas kernels, swapped(): pl.pallas_call(swap_kernel, out_shape=jax.ShapeDtypeStruct(sent.shape, se...  9.03 us
    broadcast_in_dim x1, other arithmetic, shards(): return (own + swapped(sent).astype(jnp.float32)).astype(jnp.bfloat16)[None]  2.26 us

profile of v5, /device:TPU:9, one launch (start us, length us, event | category | flops | bytes accessed | tf_op | source)
XLA Modules:
  0.0 55.5 jit_solution(894586265697374402)
XLA Ops:
  0.0 32.9 %front.1 = (bf16[6,16,256,128]{3,2,1,0:T(8,128)(2,1)}, f32[16,256,128]{2,1,0:T(8,128)}) custom-call(s32[17]{0:T(128)} %class_ref.3, bf16[16,256,128]{2,1,0:T(8,128)(2,1)} %bitcast.8, bf16[17,256,256]{2,1,0:T(8,128)(2,1)} %bitcast.6, bf16[17,128,128]{2,1,0:T(8,128)(2,1)} %bitcast.10, bf16[16,16,17]{2,1,0:T(8,128)(2,1)} %bitcast.12), custom_call_target="tpu_custom_call" | custom-call | tf_op jit(solution)/shard_map/front/pallas_call | solution.py:229
  32.9 11.2 %rest.1 = (f32[8,256,128]{2,1,0:T(8,128)}, bf16[8,256,128]{2,1,0:T(8,128)(2,1)}) custom-call(s32[17]{0:T(128)} %class_ref.3, bf16[16,256,128]{2,1,0:T(8,128)(2,1)} %bitcast.9, bf16[6,16,256,128]{3,2,1,0:T(8,128)(2,1)} %get-tuple-element.9.got_ref, bf16[17,256,256]{2,1,0:T(8,128)(2,1)} %bitcast.7, bf16[17,128,128]{2,1,0:T(8,128)(2,1)} %bitcast.11, ...), custom_call_target="tpu_custom_call" | custom-call | tf_op jit(solution)/shard_map/rest/pallas_call | solution.py:328
  44.2 9.0 %swap.1 = bf16[8,256,128]{2,1,0:T(8,128)(2,1)} custom-call(bf16[8,256,128]{2,1,0:T(8,128)(2,1)} %get-tuple-element.12.sent_ref), custom_call_target="tpu_custom_call" | custom-call | tf_op jit(solution)/shard_map/swap/pallas_call | solution.py:366
  53.2 2.3 %fusion = bf16[1,8,256,128]{3,2,1,0:T(8,128)(2,1)} fusion(f32[8,256,128]{2,1,0:T(8,128)} %get-tuple-element.11, bf16[8,256,128]{2,1,0:T(8,128)(2,1)} %swap.1), kind=kLoop, calls=%fused_computation.1 | loop fusion | flops 786432 | bytes 2097152 | tf_op jit(solution)/shard_map/broadcast_in_dim | solution.py:383

commit v6 on v4

--- a/solution.py
+++ b/solution.py
@@ -313,7 +313,7 @@
         )
 
     half = states // 2
-    own_ref[...] = acc[pl.ds(core * half, half)]
+    own_ref[...] = acc[pl.ds(core * half, half)].astype(own_ref.dtype)
     sent_ref[...] = acc[pl.ds((1 - core) * half, half)].astype(sent_ref.dtype)
 
 
@@ -323,7 +323,7 @@
     half = (states // 2, rows, width)
     return pl.pallas_call(
         functools.partial(rest_kernel, sectors),
-        out_shape=(jax.ShapeDtypeStruct(half, jnp.float32), jax.ShapeDtypeStruct(half, jnp.bfloat16)),
+        out_shape=(jax.ShapeDtypeStruct(half, jnp.bfloat16), jax.ShapeDtypeStruct(half, jnp.bfloat16)),
         in_specs=[SMEM_SPEC, ANY_SPEC, ANY_SPEC, ANY_SPEC, ANY_SPEC, VMEM_SPEC, ANY_SPEC],
         out_specs=(VMEM_SPEC, VMEM_SPEC),
         scratch_shapes=[
@@ -376,7 +376,7 @@
     mpo = jnp.transpose(mpo_local, (1, 2, 0))
     got, total = front(term_class, psi, left, right, mpo, sectors)
     own, sent = rest(term_class, psi, got, left, right, mpo, total, sectors)
-    return (own + swapped(sent).astype(jnp.float32)).astype(jnp.bfloat16)[None]
+    return (own.astype(jnp.float32) + swapped(sent).astype(jnp.float32)).astype(jnp.bfloat16)[None]
 
 
 def solution(mesh):

time: 54.1 us -> 53.1 us (0.982)
  the two profiles are of different devices: /device:TPU:3 before, /device:TPU:9 now
where the time goes in v6:
time: 53.1 us; the launch traced here: 52.7 us
  Pallas kernels  50.6 us (95%)
  other arithmetic  2.14 us (4%)
    pallas_call x1, Pallas kernels, front(): pl.pallas_call(functools.partial(front_kernel, sectors), out_shape=(jax.S...  32.9 us
    pallas_call x1, Pallas kernels, rest(): pl.pallas_call(functools.partial(rest_kernel, sectors), out_shape=(jax.Sh...  15.4 us
    pallas_call x1, Pallas kernels, swapped(): pl.pallas_call(swap_kernel, out_shape=jax.ShapeDtypeStruct(sent.shape, se...  2.3 us
    broadcast_in_dim x1, other arithmetic, shards(): (own.astype(jnp.float32) + swapped(sent).astype(jnp.float32)).astype(jnp....  2.14 us

profile of v6, /device:TPU:9, one launch (start us, length us, event | category | flops | bytes accessed | tf_op | source)
XLA Modules:
  0.0 52.7 jit_solution(9360731925932201213)
XLA Ops:
  0.0 32.9 %front.1 = (bf16[6,16,256,128]{3,2,1,0:T(8,128)(2,1)}, f32[16,256,128]{2,1,0:T(8,128)}) custom-call(s32[17]{0:T(128)} %class_ref.3, bf16[16,256,128]{2,1,0:T(8,128)(2,1)} %bitcast.8, bf16[17,256,256]{2,1,0:T(8,128)(2,1)} %bitcast.6, bf16[17,128,128]{2,1,0:T(8,128)(2,1)} %bitcast.10, bf16[16,16,17]{2,1,0:T(8,128)(2,1)} %bitcast.12), custom_call_target="tpu_custom_call" | custom-call | tf_op jit(solution)/shard_map/front/pallas_call | solution.py:228
  32.9 15.4 %rest.1 = (bf16[8,256,128]{2,1,0:T(8,128)(2,1)}, bf16[8,256,128]{2,1,0:T(8,128)(2,1)}) custom-call(s32[17]{0:T(128)} %class_ref.3, bf16[16,256,128]{2,1,0:T(8,128)(2,1)} %bitcast.9, bf16[6,16,256,128]{3,2,1,0:T(8,128)(2,1)} %get-tuple-element.9.got_ref, bf16[17,256,256]{2,1,0:T(8,128)(2,1)} %bitcast.7, bf16[17,128,128]{2,1,0:T(8,128)(2,1)} %bitcast.11, ...), custom_call_target="tpu_custom_call" | custom-call | tf_op jit(solution)/shard_map/rest/pallas_call | solution.py:324
  48.3 2.3 %swap.1 = bf16[8,256,128]{2,1,0:T(8,128)(2,1)} custom-call(bf16[8,256,128]{2,1,0:T(8,128)(2,1)} %get-tuple-element.12.sent_ref), custom_call_target="tpu_custom_call" | custom-call | tf_op jit(solution)/shard_map/swap/pallas_call | solution.py:362
  50.6 2.1 %fusion = bf16[1,8,256,128]{3,2,1,0:T(8,128)(2,1)} fusion(bf16[8,256,128]{2,1,0:T(8,128)(2,1)} %swap.1, bf16[8,256,128]{2,1,0:T(8,128)(2,1)} %get-tuple-element.11), kind=kLoop, calls=%fused_computation.1 | loop fusion | flops 1048576 | bytes 1572864 | tf_op jit(solution)/shard_map/broadcast_in_dim | solution.py:379
